TPU v7x, 32 devices: a whole 2x2x4 slice. The times are simulated.
32 devices in a mesh: slab: 32 (over z, y, x, core).
Axes of the slice: x: 2, y: 2, z: 4, core: 2. Of those that a mesh axis runs over, the one named last changes fastest.
Arguments:
- velocity: bfloat16 [3, 128, 16, 4096], P(None, 'slab'), may hold values from -6 to 6
Outputs:
- composite: float32 [4, 32768], P(None, 'slab')
All inputs are finite; a program needn't handle non-finite values.
Results may differ from a plain program's by a relative error of at most 0.00085.
Values may be sent and summed in bfloat16 or wider, within the bound.
A program may use at most 192 MiB of HBM per device.

v0:
```python
import functools

import jax
import jax.numpy as jnp
import ml_dtypes
import numpy as np
from jax import lax
from jax.experimental import pallas as pl
from jax.experimental.pallas import tpu as pltpu
from jax.sharding import PartitionSpec as P

MESH = pl.DeviceIdType.MESH
opacity_gain = 5.0

smooth_taps = np.array([1, 4, 6, 4, 1]) / 16.0
slope_taps = np.array([1, -8, 0, 8, -1]) / 1.0
both_taps = np.convolve(smooth_taps, slope_taps)
CZ, YH, BAND = 4, 16, 8
KEEP = YH - 4
FIELDS = 6
LANE = 128
SIDE = 96
MARGIN = 256
CHUNK = 1024


def halo_row(component, plane, row):
    below = plane < 0
    source = plane + CZ if below else plane - CZ
    spec, band = (0, 32) if below else (SIDE + 64, SIDE)
    near = source - 2 if below else source
    if component < 2 and 2 <= row < 2 + BAND:
        return band + 32 * component + source * BAND + row - 2
    assert component != 1 and 0 <= near < 2
    if component == 0:
        return spec + near * 4 + (row if row < 2 else row - BAND)
    return spec + 8 + near * KEEP + row


def weights():
    send = np.zeros((128, 192))
    own = np.zeros((FIELDS * 32, 192))
    halo = np.zeros((FIELDS * 32, 192))

    def put(at, component, source, row):
        for b in range(5):
            send[at, component * 64 + source * YH + row + b] += smooth_taps[b]

    for component in range(2):
        for source in range(CZ):
            for r in range(BAND):
                put(32 + 32 * component + source * BAND + r, component, source, r + 2)
    for start, planes in ((0, (2, 3)), (96, (0, 1))):
        for near, source in enumerate(planes):
            for i, row in enumerate((0, 1, 10, 11)):
                put(start + near * 4 + i, 0, source, row)
            for row in range(KEEP):
                put(start + 8 + near * KEEP + row, 2, source, row)

    def term(field, component, z_taps, y_slope, sign):
        y_own = both_taps if y_slope else smooth_taps
        y_halo = slope_taps if y_slope else np.ones(1)
        for p in range(CZ):
            for r in range(BAND):
                at = field * 32 + p * BAND + r
                for a, wz in enumerate(z_taps):
                    plane = p + a - len(z_taps) // 2
                    if wz == 0:
                        continue
                    if 0 <= plane < CZ:
                        for b, wy in enumerate(y_own):
                            row = r + 4 + b - len(y_own) // 2
                            own[at, component * 64 + plane * YH + row] += sign * wz * wy / 16.0
                    else:
                        for b, wy in enumerate(y_halo):
                            if wy:
                                row = r + 2 + b - len(y_halo) // 2
                                halo[at, halo_row(component, plane, row)] += sign * wz * wy / 16.0

    term(0, 2, smooth_taps, True, 1.0)
    term(0, 1, both_taps, False, -1.0)
    term(1, 0, both_taps, False, 1.0)
    term(2, 0, smooth_taps, True, 1.0)
    for k in range(3):
        term(3 + k, k, smooth_taps, False, 1.0)
    full = np.concatenate([send, own, halo], axis=0)
    rounded = full.astype(ml_dtypes.bfloat16)
    assert np.all(rounded.astype(np.float64) == full)
    return rounded


def shift(field, by):
    return pltpu.roll(field, by % field.shape[1], 1)


def smooth_x(field):
    for _ in range(2):
        field = field + shift(field, 1)
        field = field + shift(field, -1)
    return field


def slope_x(field):
    near = shift(field, -1) - shift(field, 1)
    return 8.0 * near - (shift(near, 1) + shift(near, -1))


def spans(nx):
    chunks = nx // CHUNK
    cuts = [[(nx - MARGIN, MARGIN), (0, CHUNK + MARGIN)]]
    for c in range(1, chunks):
        first = c * CHUNK + MARGIN
        cuts.append([(first, min(CHUNK, nx - MARGIN - first))])
    return cuts


def kernel(n, exchange, nx, raw, mats, out, send, halo, fields, *rest):
    if exchange:
        staged, outbox, inbox, up_s, up_r, down_s, down_r, out_s, in_r = rest
    else:
        up_s, up_r, down_s, down_r = rest
    me = lax.axis_index("slab")
    up, down = lax.rem(me + 1, n), lax.rem(me + n - 1, n)
    barrier = pltpu.get_barrier_semaphore()
    cuts = spans(nx)
    pieces = [(c, i, first, width) for c, cut in enumerate(cuts) for i, (first, width) in enumerate(cut)]
    number = {(c, i): k for k, (c, i, _, _) in enumerate(pieces)}

    if exchange:
        def greet(hop, _):
            pl.semaphore_signal(barrier, inc=1, device_id=(lax.rem(me + hop, n),), device_id_type=MESH)
            return 0

        lax.fori_loop(1, n, greet, 0)
    else:
        for other in (up, down):
            pl.semaphore_signal(barrier, inc=1, device_id=(other,), device_id_type=MESH)

    def halo_copies(k):
        _, _, first, width = pieces[k]
        lanes = pl.ds(first, width)
        return (
            pltpu.make_async_remote_copy(
                src_ref=send.at[pl.ds(0, SIDE), lanes], dst_ref=halo.at[pl.ds(0, SIDE), lanes],
                send_sem=up_s.at[k], recv_sem=up_r.at[k], device_id=(up,), device_id_type=MESH),
            pltpu.make_async_remote_copy(
                src_ref=send.at[pl.ds(32, SIDE), lanes], dst_ref=halo.at[pl.ds(SIDE, SIDE), lanes],
                send_sem=down_s.at[k], recv_sem=down_r.at[k], device_id=(down,), device_id_type=MESH),
        )

    for k, (_, _, first, width) in enumerate(pieces):
        send[:, pl.ds(first, width)] = jnp.dot(
            mats[0:128, :], raw[:, pl.ds(first, width)], preferred_element_type=jnp.float32
        ).astype(jnp.bfloat16)
        if k == 0:
            pl.semaphore_wait(barrier, n - 1 if exchange else 2)
        for copy in halo_copies(k):
            copy.start()

    def places(first, width):
        here = [(first + MARGIN, 0, width)]
        if first == 0:
            here.append((nx + MARGIN, 0, MARGIN))
        if first + width == nx:
            here.append((0, width - MARGIN, MARGIN))
        return here

    for _, _, first, width in pieces:
        own = jnp.dot(mats[128:320, :], raw[:, pl.ds(first, width)], preferred_element_type=jnp.float32)
        fields[:, pl.ds(first + MARGIN, width)] = own

    def add_halo(first, width):
        more = jnp.dot(mats[320:512, :], halo[:, pl.ds(first, width)], preferred_element_type=jnp.float32)
        total = fields[:, pl.ds(first + MARGIN, width)] + more
        for at, skip, size in places(first, width):
            fields[:, pl.ds(at, size)] = total[:, skip:skip + size]

    scale = opacity_gain / (144.0 * CZ * n)
    for c, cut in enumerate(cuts):
        for i, (first, width) in enumerate(cut):
            for copy in halo_copies(number[(c, i)]):
                copy.wait_recv()
            add_halo(first, width)
        begin = MARGIN + c * CHUNK - LANE
        window = pl.ds(begin, CHUNK + 2 * LANE)

        def centre(field):
            return field[:, LANE:LANE + CHUNK]

        through = None
        for p in range(CZ):
            def load(field):
                return fields[field * 32 + p * BAND:field * 32 + (p + 1) * BAND, window]

            ux = centre(smooth_x(load(3)))
            uy = smooth_x(load(4))
            uz = smooth_x(load(5))
            curl = centre(smooth_x(load(0)))
            square = curl * curl
            curl = centre(smooth_x(load(1)) - slope_x(uz))
            square += curl * curl
            curl = centre(slope_x(uy) - smooth_x(load(2)))
            density = (square + curl * curl) * scale
            left = jnp.exp(-density)
            tinted = [jnp.tanh(u) for u in (ux, centre(uy), centre(uz))]
            if through is None:
                weight = 1.0 - left
                through, depth = left, density
                sums = [weight * u for u in tinted]
            else:
                weight = through * (1.0 - left)
                through, depth = through * left, depth + density
                sums = [s + weight * u for s, u in zip(sums, tinted)]
        parts = sums + [depth]
        if not exchange:
            for q, part in enumerate(parts):
                out[q, :, pl.ds(c * CHUNK, CHUNK)] = part
            continue
        for q, part in enumerate(parts):
            for j in range(8):
                staged[:, q * 8 + j, :] = part[:, j * LANE:(j + 1) * LANE]
        outbox[pl.ds(c * BAND, BAND)] = staged[...].astype(jnp.bfloat16)

        def post(r, _):
            owner = r * (nx // CHUNK) + c

            @pl.when(owner != me)
            def _():
                pltpu.make_async_remote_copy(
                    src_ref=outbox.at[c * BAND + r], dst_ref=inbox.at[me], send_sem=out_s.at[owner],
                    recv_sem=in_r.at[me], device_id=(owner,), device_id_type=MESH).start()

            @pl.when(owner == me)
            def _():
                inbox[me] = outbox[c * BAND + r]

            return 0

        lax.fori_loop(0, BAND, post, 0)

    if exchange:
        def arrived(hop, _):
            source = lax.rem(me + hop, n)
            pltpu.make_async_remote_copy(
                src_ref=outbox.at[0], dst_ref=inbox.at[source], send_sem=out_s.at[source],
                recv_sem=in_r.at[source], device_id=(source,), device_id_type=MESH).wait_recv()
            return 0

        lax.fori_loop(1, n, arrived, 0)
        through = jnp.ones((8, LANE), jnp.float32)
        total = [jnp.zeros((8, LANE), jnp.float32) for _ in range(3)]
        for s in range(n):
            block = inbox[s].astype(jnp.float32)
            left = jnp.exp(-block[24:32])
            half = 0.5 * through
            cover = 1.0 - left
            total = [t + half * (cover + block[q * 8:q * 8 + 8]) for q, t in enumerate(total)]
            through = through * left
        total.append(1.0 - through)
        for q, value in enumerate(total):
            for j in range(8):
                out[q:q + 1, pl.ds(j * LANE, LANE)] = value[j:j + 1, :]

        def left_home(hop, _):
            other = lax.rem(me + hop, n)
            pltpu.make_async_remote_copy(
                src_ref=outbox.at[0], dst_ref=inbox.at[me], send_sem=out_s.at[other],
                recv_sem=in_r.at[me], device_id=(other,), device_id_type=MESH).wait_send()
            return 0

        lax.fori_loop(1, n, left_home, 0)
    for k in range(len(pieces)):
        for copy in halo_copies(k):
            copy.wait_send()


def per_device(velocity):
    n = lax.axis_size("slab")
    nx = velocity.shape[3]
    pixels = BAND * nx // n
    exchange = pixels == CHUNK
    pieces = sum(len(cut) for cut in spans(nx))
    bf16, f32 = jnp.bfloat16, jnp.float32
    scratch = [
        pltpu.VMEM((128, nx), bf16),
        pltpu.VMEM((2 * SIDE, nx), bf16),
        pltpu.VMEM((FIELDS * 32, nx + 2 * MARGIN), f32),
    ]
    if exchange:
        scratch += [
            pltpu.VMEM((BAND, 32, LANE), f32),
            pltpu.VMEM((n, 32, LANE), bf16),
            pltpu.VMEM((n, 32, LANE), bf16),
        ]
    scratch += [pltpu.SemaphoreType.DMA((pieces,))] * 4
    if exchange:
        scratch += [pltpu.SemaphoreType.DMA((n,))] * 2
    shape = (4, pixels) if exchange else (4, BAND, nx)
    result = pl.pallas_call(
        functools.partial(kernel, n, exchange, nx),
        out_shape=jax.ShapeDtypeStruct(shape, f32),
        in_specs=[pl.BlockSpec(memory_space=pltpu.VMEM)] * 2,
        out_specs=pl.BlockSpec(memory_space=pltpu.VMEM),
        scratch_shapes=scratch,
        compiler_params=pltpu.CompilerParams(
            collective_id=0, has_side_effects=True, vmem_limit_bytes=48 * 1024 * 1024
        ),
    )(velocity.reshape(3 * CZ * YH, nx), jnp.asarray(weights()))
    if exchange:
        return result
    parts = result.reshape(4, n, pixels).transpose(1, 0, 2).astype(bf16)
    parts = lax.all_to_all(parts, "slab", 0, 0, tiled=True).astype(f32)
    depth = parts[:, 3]
    before = jnp.exp(-(jnp.cumsum(depth, axis=0) - depth))
    cover = 1.0 - jnp.exp(-depth)
    colours = jnp.sum(0.5 * before[:, None] * (cover[:, None] + parts[:, :3]), axis=0)
    return jnp.concatenate([colours, (1.0 - jnp.exp(-jnp.sum(depth, axis=0)))[None]], axis=0)


def solution(mesh):
    return jax.shard_map(
        per_device, mesh=mesh, in_specs=(P(None, "slab", None, None),), out_specs=P(None, "slab"), check_vma=False
    )
```

profile of v0, /device:TPU:3, one launch (start us, length us, event | category | flops | bytes accessed | tf_op | source)
XLA Modules:
  0.0 42.8 jit_solution(12970263167494930686)
XLA Ops:
  0.0 0.0 copy-start
  0.0 1.4 %copy-done = bf16[3,4,16,4096]{3,2,1,0:T(8,128)(2,1)S(1)} copy-done((bf16[3,4,16,4096]{3,2,1,0:T(8,128)(2,1)S(1)}, bf16[3,4,16,4096]{3,2,1,0:T(8,128)(2,1)}, u32[]{:S(2)}) %copy-start) | copy-done | bytes 1572888
  1.4 0.0 copy-start.1
  1.4 0.9 %copy-done.1 = bf16[512,192]{1,0:T(8,128)(2,1)S(1)} copy-done((bf16[512,192]{1,0:T(8,128)(2,1)S(1)}, bf16[512,192]{1,0:T(8,128)(2,1)}, u32[]{:S(2)}) %copy-start.1) | copy-done | bytes 196632
  2.4 39.8 %shard_map.28 = f32[4,1024]{1,0:T(4,128)S(1)} custom-call(bf16[192,4096]{1,0:T(8,128)(2,1)S(1)} %bitcast.1, bf16[512,192]{1,0:T(8,128)(2,1)S(1)} %copy-done.1), custom_call_target="tpu_custom_call" | custom-call | tf_op jit(solution)/shard_map/pallas_call | solution.py:299
  42.2 0.6 %copy.4 = f32[4,1024]{1,0:T(4,128)} copy(f32[4,1024]{1,0:T(4,128)S(1)} %shard_map.28) | data formatting | bytes 32768
Async XLA Ops:
  0.0 1.4 %copy-start = (bf16[3,4,16,4096]{3,2,1,0:T(8,128)(2,1)S(1)}, bf16[3,4,16,4096]{3,2,1,0:T(8,128)(2,1)}, u32[]{:S(2)}) copy-start(bf16[3,4,16,4096]{3,2,1,0:T(8,128)(2,1)} %param.2) | copy-start | bytes 4718596
  1.4 0.9 %copy-start.1 = (bf16[512,192]{1,0:T(8,128)(2,1)S(1)}, bf16[512,192]{1,0:T(8,128)(2,1)}, u32[]{:S(2)}) copy-start(bf16[512,192]{1,0:T(8,128)(2,1)} %constant.2.clone.mats) | copy-start | bytes 589828
where the time goes:
time: 42.9 us; the launch traced here: 42.8 us
  Pallas kernels  39.8 us (93%)
  local copies, waits for them, and re-layouts  2.96 us (7%)
    pallas_call x1, Pallas kernels, per_device(): pl.pallas_call(functools.partial(kernel, n, exchange, nx), out_shape=jax....  39.8 us
    unnamed x5, local copies, waits for them, and re-layouts  2.96 us

commit v1 on v0

--- a/solution.py
+++ b/solution.py
@@ -20,8 +20,9 @@
 FIELDS = 6
 LANE = 128
 SIDE = 96
-MARGIN = 256
 CHUNK = 1024
+TILE = 512
+CELL = 256
 
 
 def halo_row(component, plane, row):
@@ -105,27 +106,22 @@
     return 8.0 * near - (shift(near, 1) + shift(near, -1))
 
 
-def spans(nx):
-    chunks = nx // CHUNK
-    cuts = [[(nx - MARGIN, MARGIN), (0, CHUNK + MARGIN)]]
-    for c in range(1, chunks):
-        first = c * CHUNK + MARGIN
-        cuts.append([(first, min(CHUNK, nx - MARGIN - first))])
-    return cuts
-
-
-def kernel(n, exchange, nx, raw, mats, out, send, halo, fields, *rest):
-    if exchange:
-        staged, outbox, inbox, up_s, up_r, down_s, down_r, out_s, in_r = rest
+def kernel(n, exchange, nx, raw_hbm, mats, out, raw, send, halo, fields, *rest):
+    if exchange:
+        staged, outbox, inbox, in_s, up_s, up_r, down_s, down_r, out_s, in_r = rest
     else:
-        up_s, up_r, down_s, down_r = rest
+        in_s, up_s, up_r, down_s, down_r = rest
     me = lax.axis_index("slab")
     up, down = lax.rem(me + 1, n), lax.rem(me + n - 1, n)
     barrier = pltpu.get_barrier_semaphore()
-    cuts = spans(nx)
-    pieces = [(c, i, first, width) for c, cut in enumerate(cuts) for i, (first, width) in enumerate(cut)]
-    number = {(c, i): k for k, (c, i, _, _) in enumerate(pieces)}
-
+    chunks, tiles, cells = nx // CHUNK, nx // TILE, nx // CELL
+
+    inward = [
+        pltpu.make_async_copy(raw_hbm.at[:, pl.ds(first, width)], raw.at[:, pl.ds(at, width)], in_s.at[i])
+        for i, (first, width, at) in enumerate(((nx - LANE, LANE, 0), (0, LANE, nx + LANE), (0, nx, LANE)))
+    ]
+    for copy in inward:
+        copy.start()
     if exchange:
         def greet(hop, _):
             pl.semaphore_signal(barrier, inc=1, device_id=(lax.rem(me + hop, n),), device_id_type=MESH)
@@ -136,8 +132,13 @@
         for other in (up, down):
             pl.semaphore_signal(barrier, inc=1, device_id=(other,), device_id_type=MESH)
 
+    pieces = [(nx - CELL, CELL, 1, 0), (0, TILE, 2, 0), (TILE, CHUNK + CELL - TILE, 4, 0)]
+    for c in range(1, chunks):
+        first = c * CHUNK + CELL
+        pieces.append((first, min(CHUNK, nx - CELL - first), min(4 + 2 * c, tiles), c))
+
     def halo_copies(k):
-        _, _, first, width = pieces[k]
+        first, width, _, _ = pieces[k]
         lanes = pl.ds(first, width)
         return (
             pltpu.make_async_remote_copy(
@@ -148,61 +149,70 @@
                 send_sem=down_s.at[k], recv_sem=down_r.at[k], device_id=(down,), device_id_type=MESH),
         )
 
-    for k, (_, _, first, width) in enumerate(pieces):
-        send[:, pl.ds(first, width)] = jnp.dot(
-            mats[0:128, :], raw[:, pl.ds(first, width)], preferred_element_type=jnp.float32
-        ).astype(jnp.bfloat16)
-        if k == 0:
-            pl.semaphore_wait(barrier, n - 1 if exchange else 2)
-        for copy in halo_copies(k):
-            copy.start()
-
-    def places(first, width):
-        here = [(first + MARGIN, 0, width)]
-        if first == 0:
-            here.append((nx + MARGIN, 0, MARGIN))
-        if first + width == nx:
-            here.append((0, width - MARGIN, MARGIN))
-        return here
-
-    for _, _, first, width in pieces:
-        own = jnp.dot(mats[128:320, :], raw[:, pl.ds(first, width)], preferred_element_type=jnp.float32)
-        fields[:, pl.ds(first + MARGIN, width)] = own
-
-    def add_halo(first, width):
-        more = jnp.dot(mats[320:512, :], halo[:, pl.ds(first, width)], preferred_element_type=jnp.float32)
-        total = fields[:, pl.ds(first + MARGIN, width)] + more
-        for at, skip, size in places(first, width):
-            fields[:, pl.ds(at, size)] = total[:, skip:skip + size]
+    def filtered(rows, first):
+        window = raw[:, pl.ds(first, TILE + 2 * LANE)]
+        return smooth_x(jnp.dot(mats[rows, :], window, preferred_element_type=jnp.float32))[:, LANE:LANE + TILE]
+
+    def to_send(k, _):
+        first = pl.multiple_of(lax.rem(k + tiles - 1, tiles) * TILE, TILE)
+        send[:, pl.ds(first, TILE)] = filtered(slice(0, 128), first).astype(jnp.bfloat16)
+        for i, (_, _, ready, _) in enumerate(pieces):
+            @pl.when(k == ready - 1)
+            def _():
+                for copy in halo_copies(i):
+                    copy.start()
+        return 0
+
+    for copy in inward:
+        copy.wait()
+    pl.semaphore_wait(barrier, n - 1 if exchange else 2)
+    lax.fori_loop(0, tiles, to_send, 0)
+
+    def own(k, _):
+        first = pl.multiple_of(k * TILE, TILE)
+        fields[:, pl.ds(first + LANE, TILE)] = filtered(slice(128, 320), first)
+        return 0
+
+    lax.fori_loop(0, tiles, own, 0)
+
+    def add_halo(k, _):
+        first = pl.multiple_of(lax.rem(k + cells - 1, cells) * CELL, CELL)
+        more = jnp.dot(mats[320:512, :], halo[:, pl.ds(first, CELL)], preferred_element_type=jnp.float32)
+        total = fields[:, pl.ds(first + LANE, CELL)] + more
+        fields[:, pl.ds(first + LANE, CELL)] = total
+
+        @pl.when(first == 0)
+        def _():
+            fields[128:192, nx + LANE:nx + 2 * LANE] = total[128:192, 0:LANE]
+
+        @pl.when(first == nx - CELL)
+        def _():
+            fields[128:192, 0:LANE] = total[128:192, CELL - LANE:CELL]
+
+        return 0
 
     scale = opacity_gain / (144.0 * CZ * n)
-    for c, cut in enumerate(cuts):
-        for i, (first, width) in enumerate(cut):
-            for copy in halo_copies(number[(c, i)]):
-                copy.wait_recv()
-            add_halo(first, width)
-        begin = MARGIN + c * CHUNK - LANE
-        window = pl.ds(begin, CHUNK + 2 * LANE)
-
-        def centre(field):
-            return field[:, LANE:LANE + CHUNK]
-
+    per_chunk = CHUNK // CELL
+
+    def shade(k, _):
+        first = pl.multiple_of(k * CELL, CELL)
         through = None
         for p in range(CZ):
-            def load(field):
-                return fields[field * 32 + p * BAND:field * 32 + (p + 1) * BAND, window]
-
-            ux = centre(smooth_x(load(3)))
-            uy = smooth_x(load(4))
-            uz = smooth_x(load(5))
-            curl = centre(smooth_x(load(0)))
+            def centre(field):
+                return fields[field * 32 + p * BAND:field * 32 + (p + 1) * BAND, pl.ds(first + LANE, CELL)]
+
+            def slope(field):
+                window = fields[field * 32 + p * BAND:field * 32 + (p + 1) * BAND, pl.ds(first, CELL + 2 * LANE)]
+                return slope_x(window)[:, LANE:LANE + CELL]
+
+            curl = centre(0)
             square = curl * curl
-            curl = centre(smooth_x(load(1)) - slope_x(uz))
+            curl = centre(1) - slope(5)
             square += curl * curl
-            curl = centre(slope_x(uy) - smooth_x(load(2)))
+            curl = slope(4) - centre(2)
             density = (square + curl * curl) * scale
             left = jnp.exp(-density)
-            tinted = [jnp.tanh(u) for u in (ux, centre(uy), centre(uz))]
+            tinted = [jnp.tanh(centre(3 + q)) for q in range(3)]
             if through is None:
                 weight = 1.0 - left
                 through, depth = left, density
@@ -211,18 +221,32 @@
                 weight = through * (1.0 - left)
                 through, depth = through * left, depth + density
                 sums = [s + weight * u for s, u in zip(sums, tinted)]
-        parts = sums + [depth]
+        for q, part in enumerate(sums + [depth]):
+            if not exchange:
+                out[q, :, pl.ds(first, CELL)] = part
+                continue
+            for j in range(CELL // LANE):
+                row = q * 8 + lax.rem(k, per_chunk) * (CELL // LANE) + j
+                staged[pl.ds(pl.multiple_of(row * BAND, BAND), BAND), :] = part[:, j * LANE:(j + 1) * LANE]
+        return 0
+
+    def one_chunk(c, _):
+        for i, (_, _, _, chunk) in enumerate(pieces):
+            @pl.when(c == chunk)
+            def _():
+                for copy in halo_copies(i):
+                    copy.wait_recv()
+
+        begin = jnp.where(c == 0, 0, c * per_chunk + 2)
+        lax.fori_loop(begin, jnp.minimum((c + 1) * per_chunk + 2, cells), add_halo, 0)
+        lax.fori_loop(c * per_chunk, (c + 1) * per_chunk, shade, 0)
         if not exchange:
-            for q, part in enumerate(parts):
-                out[q, :, pl.ds(c * CHUNK, CHUNK)] = part
-            continue
-        for q, part in enumerate(parts):
-            for j in range(8):
-                staged[:, q * 8 + j, :] = part[:, j * LANE:(j + 1) * LANE]
-        outbox[pl.ds(c * BAND, BAND)] = staged[...].astype(jnp.bfloat16)
+            return 0
+        for r in range(BAND):
+            outbox[c * BAND + r] = staged[pl.ds(r, 32, stride=BAND), :].astype(jnp.bfloat16)
 
         def post(r, _):
-            owner = r * (nx // CHUNK) + c
+            owner = r * chunks + c
 
             @pl.when(owner != me)
             def _():
@@ -237,6 +261,9 @@
             return 0
 
         lax.fori_loop(0, BAND, post, 0)
+        return 0
+
+    lax.fori_loop(0, chunks, one_chunk, 0)
 
     if exchange:
         def arrived(hop, _):
@@ -279,19 +306,21 @@
     nx = velocity.shape[3]
     pixels = BAND * nx // n
     exchange = pixels == CHUNK
-    pieces = sum(len(cut) for cut in spans(nx))
+    pieces = 2 + nx // CHUNK
     bf16, f32 = jnp.bfloat16, jnp.float32
     scratch = [
+        pltpu.VMEM((192, nx + 2 * LANE), bf16),
         pltpu.VMEM((128, nx), bf16),
         pltpu.VMEM((2 * SIDE, nx), bf16),
-        pltpu.VMEM((FIELDS * 32, nx + 2 * MARGIN), f32),
+        pltpu.VMEM((FIELDS * 32, nx + 2 * LANE), f32),
     ]
     if exchange:
         scratch += [
-            pltpu.VMEM((BAND, 32, LANE), f32),
+            pltpu.VMEM((32 * BAND, LANE), f32),
             pltpu.VMEM((n, 32, LANE), bf16),
             pltpu.VMEM((n, 32, LANE), bf16),
         ]
+    scratch += [pltpu.SemaphoreType.DMA((3,))]
     scratch += [pltpu.SemaphoreType.DMA((pieces,))] * 4
     if exchange:
         scratch += [pltpu.SemaphoreType.DMA((n,))] * 2
@@ -299,7 +328,7 @@
     result = pl.pallas_call(
         functools.partial(kernel, n, exchange, nx),
         out_shape=jax.ShapeDtypeStruct(shape, f32),
-        in_specs=[pl.BlockSpec(memory_space=pltpu.VMEM)] * 2,
+        in_specs=[pl.BlockSpec(memory_space=pl.ANY), pl.BlockSpec(memory_space=pltpu.VMEM)],
         out_specs=pl.BlockSpec(memory_space=pltpu.VMEM),
         scratch_shapes=scratch,
         compiler_params=pltpu.CompilerParams(

time: 42.9 us -> 36.2 us (0.84)
  Pallas kernels: 39.8 us -> 33.1 us
    pallas_call x1, Pallas kernels: 39.8 us -> 33.1 us  [per_device(): pl.pallas_call(functools.partial(kernel, n, exchange, nx), out_shape=jax....]
where the time goes in v1:
time: 36.2 us; the launch traced here: 36 us
  Pallas kernels  33.1 us (91%)
  local copies, waits for them, and re-layouts  2.96 us (8%)
    pallas_call x1, Pallas kernels, per_device(): pl.pallas_call(functools.partial(kernel, n, exchange, nx), out_shape=jax....  33.1 us
    unnamed x5, local copies, waits for them, and re-layouts  2.96 us

profile of v1, /device:TPU:3, one launch (start us, length us, event | category | flops | bytes accessed | tf_op | source)
XLA Modules:
  0.0 36.0 jit_solution(1721769801709090573)
XLA Ops:
  0.0 0.0 copy-start
  0.0 1.4 %copy-done = bf16[3,4,16,4096]{3,2,1,0:T(8,128)(2,1)S(1)} copy-done((bf16[3,4,16,4096]{3,2,1,0:T(8,128)(2,1)S(1)}, bf16[3,4,16,4096]{3,2,1,0:T(8,128)(2,1)}, u32[]{:S(2)}) %copy-start) | copy-done | bytes 1572888
  1.4 0.0 copy-start.1
  1.4 0.9 %copy-done.1 = bf16[512,192]{1,0:T(8,128)(2,1)S(1)} copy-done((bf16[512,192]{1,0:T(8,128)(2,1)S(1)}, bf16[512,192]{1,0:T(8,128)(2,1)}, u32[]{:S(2)}) %copy-start.1) | copy-done | bytes 196632
  2.4 33.1 %shard_map.28 = f32[4,1024]{1,0:T(4,128)S(1)} custom-call(bf16[192,4096]{1,0:T(8,128)(2,1)S(1)} %bitcast.1, bf16[512,192]{1,0:T(8,128)(2,1)S(1)} %copy-done.1), custom_call_target="tpu_custom_call" | custom-call | tf_op jit(solution)/shard_map/pallas_call | solution.py:328
  35.4 0.6 %copy.4 = f32[4,1024]{1,0:T(4,128)} copy(f32[4,1024]{1,0:T(4,128)S(1)} %shard_map.28) | data formatting | bytes 32768
Async XLA Ops:
  0.0 1.4 %copy-start = (bf16[3,4,16,4096]{3,2,1,0:T(8,128)(2,1)S(1)}, bf16[3,4,16,4096]{3,2,1,0:T(8,128)(2,1)}, u32[]{:S(2)}) copy-start(bf16[3,4,16,4096]{3,2,1,0:T(8,128)(2,1)} %param.2) | copy-start | bytes 4718596
  1.4 0.9 %copy-start.1 = (bf16[512,192]{1,0:T(8,128)(2,1)S(1)}, bf16[512,192]{1,0:T(8,128)(2,1)}, u32[]{:S(2)}) copy-start(bf16[512,192]{1,0:T(8,128)(2,1)} %constant.2.clone.mats) | copy-start | bytes 589828

commit v2 on v1

--- a/solution.py
+++ b/solution.py
@@ -23,6 +23,7 @@
 CHUNK = 1024
 TILE = 512
 CELL = 256
+FLIGHT = 4
 
 
 def halo_row(component, plane, row):
@@ -106,7 +107,7 @@
     return 8.0 * near - (shift(near, 1) + shift(near, -1))
 
 
-def kernel(n, exchange, nx, raw_hbm, mats, out, raw, send, halo, fields, *rest):
+def kernel(n, exchange, nx, raw_hbm, mats_hbm, out, raw, mats, send, halo, fields, *rest):
     if exchange:
         staged, outbox, inbox, in_s, up_s, up_r, down_s, down_r, out_s, in_r = rest
     else:
@@ -116,10 +117,15 @@
     barrier = pltpu.get_barrier_semaphore()
     chunks, tiles, cells = nx // CHUNK, nx // TILE, nx // CELL
 
-    inward = [
-        pltpu.make_async_copy(raw_hbm.at[:, pl.ds(first, width)], raw.at[:, pl.ds(at, width)], in_s.at[i])
-        for i, (first, width, at) in enumerate(((nx - LANE, LANE, 0), (0, LANE, nx + LANE), (0, nx, LANE)))
-    ]
+    inward = [pltpu.make_async_copy(mats_hbm, mats, in_s.at[0])]
+    for i, (first, width, at) in enumerate((
+        (nx - CELL - LANE, LANE + CELL, 0),
+        (0, CHUNK, LANE + CELL),
+        (CHUNK, nx - CELL - CHUNK, LANE + CELL + CHUNK),
+        (nx - CELL, LANE, LANE + nx),
+    )):
+        inward.append(pltpu.make_async_copy(
+            raw_hbm.at[:, pl.ds(first, width)], raw.at[:, pl.ds(at, width)], in_s.at[i + 1]))
     for copy in inward:
         copy.start()
     if exchange:
@@ -132,14 +138,8 @@
         for other in (up, down):
             pl.semaphore_signal(barrier, inc=1, device_id=(other,), device_id_type=MESH)
 
-    pieces = [(nx - CELL, CELL, 1, 0), (0, TILE, 2, 0), (TILE, CHUNK + CELL - TILE, 4, 0)]
-    for c in range(1, chunks):
-        first = c * CHUNK + CELL
-        pieces.append((first, min(CHUNK, nx - CELL - first), min(4 + 2 * c, tiles), c))
-
     def halo_copies(k):
-        first, width, _, _ = pieces[k]
-        lanes = pl.ds(first, width)
+        lanes = pl.ds(pl.multiple_of(k * TILE, TILE), TILE)
         return (
             pltpu.make_async_remote_copy(
                 src_ref=send.at[pl.ds(0, SIDE), lanes], dst_ref=halo.at[pl.ds(0, SIDE), lanes],
@@ -154,29 +154,47 @@
         return smooth_x(jnp.dot(mats[rows, :], window, preferred_element_type=jnp.float32))[:, LANE:LANE + TILE]
 
     def to_send(k, _):
-        first = pl.multiple_of(lax.rem(k + tiles - 1, tiles) * TILE, TILE)
+        first = pl.multiple_of(k * TILE, TILE)
+
+        @pl.when(k == 2)
+        def _():
+            for copy in inward[3:]:
+                copy.wait()
+
         send[:, pl.ds(first, TILE)] = filtered(slice(0, 128), first).astype(jnp.bfloat16)
-        for i, (_, _, ready, _) in enumerate(pieces):
-            @pl.when(k == ready - 1)
-            def _():
-                for copy in halo_copies(i):
-                    copy.start()
-        return 0
-
-    for copy in inward:
+
+        @pl.when(k == 0)
+        def _():
+            pl.semaphore_wait(barrier, n - 1 if exchange else 2)
+
+        @pl.when(k < FLIGHT)
+        def _():
+            for copy in halo_copies(k):
+                copy.start()
+
+        return 0
+
+    for copy in inward[:3]:
         copy.wait()
-    pl.semaphore_wait(barrier, n - 1 if exchange else 2)
     lax.fori_loop(0, tiles, to_send, 0)
 
     def own(k, _):
         first = pl.multiple_of(k * TILE, TILE)
         fields[:, pl.ds(first + LANE, TILE)] = filtered(slice(128, 320), first)
+
+        @pl.when(k + FLIGHT < tiles)
+        def _():
+            for copy in halo_copies(k):
+                copy.wait_send()
+            for copy in halo_copies(k + FLIGHT):
+                copy.start()
+
         return 0
 
     lax.fori_loop(0, tiles, own, 0)
 
     def add_halo(k, _):
-        first = pl.multiple_of(lax.rem(k + cells - 1, cells) * CELL, CELL)
+        first = pl.multiple_of(k * CELL, CELL)
         more = jnp.dot(mats[320:512, :], halo[:, pl.ds(first, CELL)], preferred_element_type=jnp.float32)
         total = fields[:, pl.ds(first + LANE, CELL)] + more
         fields[:, pl.ds(first + LANE, CELL)] = total
@@ -195,7 +213,7 @@
     per_chunk = CHUNK // CELL
 
     def shade(k, _):
-        first = pl.multiple_of(k * CELL, CELL)
+        first = pl.multiple_of(lax.rem(k + 1, cells) * CELL, CELL)
         through = None
         for p in range(CZ):
             def centre(field):
@@ -223,22 +241,24 @@
                 sums = [s + weight * u for s, u in zip(sums, tinted)]
         for q, part in enumerate(sums + [depth]):
             if not exchange:
-                out[q, :, pl.ds(first, CELL)] = part
+                out[q, :, pl.ds(pl.multiple_of(k * CELL, CELL), CELL)] = part
                 continue
             for j in range(CELL // LANE):
                 row = q * 8 + lax.rem(k, per_chunk) * (CELL // LANE) + j
                 staged[pl.ds(pl.multiple_of(row * BAND, BAND), BAND), :] = part[:, j * LANE:(j + 1) * LANE]
         return 0
 
+    per_tile = TILE // CELL
+
+    def one_tile(k, _):
+        for copy in halo_copies(k):
+            copy.wait_recv()
+        lax.fori_loop(k * per_tile, (k + 1) * per_tile, add_halo, 0)
+        return 0
+
     def one_chunk(c, _):
-        for i, (_, _, _, chunk) in enumerate(pieces):
-            @pl.when(c == chunk)
-            def _():
-                for copy in halo_copies(i):
-                    copy.wait_recv()
-
-        begin = jnp.where(c == 0, 0, c * per_chunk + 2)
-        lax.fori_loop(begin, jnp.minimum((c + 1) * per_chunk + 2, cells), add_halo, 0)
+        ready = CHUNK // TILE
+        lax.fori_loop(jnp.where(c == 0, 0, c * ready + 1), jnp.minimum((c + 1) * ready + 1, tiles), one_tile, 0)
         lax.fori_loop(c * per_chunk, (c + 1) * per_chunk, shade, 0)
         if not exchange:
             return 0
@@ -296,7 +316,7 @@
             return 0
 
         lax.fori_loop(1, n, left_home, 0)
-    for k in range(len(pieces)):
+    for k in range(tiles - FLIGHT, tiles):
         for copy in halo_copies(k):
             copy.wait_send()
 
@@ -306,10 +326,11 @@
     nx = velocity.shape[3]
     pixels = BAND * nx // n
     exchange = pixels == CHUNK
-    pieces = 2 + nx // CHUNK
+    tiles = nx // TILE
     bf16, f32 = jnp.bfloat16, jnp.float32
     scratch = [
         pltpu.VMEM((192, nx + 2 * LANE), bf16),
+        pltpu.VMEM((512, 192), bf16),
         pltpu.VMEM((128, nx), bf16),
         pltpu.VMEM((2 * SIDE, nx), bf16),
         pltpu.VMEM((FIELDS * 32, nx + 2 * LANE), f32),
@@ -320,19 +341,19 @@
             pltpu.VMEM((n, 32, LANE), bf16),
             pltpu.VMEM((n, 32, LANE), bf16),
         ]
-    scratch += [pltpu.SemaphoreType.DMA((3,))]
-    scratch += [pltpu.SemaphoreType.DMA((pieces,))] * 4
+    scratch += [pltpu.SemaphoreType.DMA((5,))]
+    scratch += [pltpu.SemaphoreType.DMA((tiles,))] * 4
     if exchange:
         scratch += [pltpu.SemaphoreType.DMA((n,))] * 2
     shape = (4, pixels) if exchange else (4, BAND, nx)
     result = pl.pallas_call(
         functools.partial(kernel, n, exchange, nx),
         out_shape=jax.ShapeDtypeStruct(shape, f32),
-        in_specs=[pl.BlockSpec(memory_space=pl.ANY), pl.BlockSpec(memory_space=pltpu.VMEM)],
+        in_specs=[pl.BlockSpec(memory_space=pl.ANY)] * 2,
         out_specs=pl.BlockSpec(memory_space=pltpu.VMEM),
         scratch_shapes=scratch,
         compiler_params=pltpu.CompilerParams(
-            collective_id=0, has_side_effects=True, vmem_limit_bytes=48 * 1024 * 1024
+            collective_id=0, has_side_effects=True, vmem_limit_bytes=60 * 1024 * 1024
         ),
     )(velocity.reshape(3 * CZ * YH, nx), jnp.asarray(weights()))
     if exchange:

time: 36.2 us -> 34.9 us (0.964)
  local copies, waits for them, and re-layouts: 2.96 us -> 1.32 us
    unnamed x5 -> x1, local copies, waits for them, and re-layouts: 2.96 us -> 1.32 us
where the time goes in v2:
time: 34.9 us; the launch traced here: 34.6 us
  Pallas kernels  33.3 us (95%)
  local copies, waits for them, and re-layouts  1.32 us (4%)
    pallas_call x1, Pallas kernels, per_device(): pl.pallas_call(functools.partial(kernel, n, exchange, nx), out_shape=jax....  33.3 us
    unnamed x1, local copies, waits for them, and re-layouts  1.32 us

profile of v2, /device:TPU:3, one launch (start us, length us, event | category | flops | bytes accessed | tf_op | source)
XLA Modules:
  0.0 34.6 jit_solution(4314766434172088493)
XLA Ops:
  0.0 33.3 %shard_map.28 = f32[4,1024]{1,0:T(4,128)} custom-call(bf16[192,4096]{1,0:T(8,128)(2,1)} %bitcast.1, bf16[512,192]{1,0:T(8,128)(2,1)} %constant.2.clone.mats_hbm), custom_call_target="tpu_custom_call" | custom-call | tf_op jit(solution)/shard_map/pallas_call | solution.py:349
  33.3 1.3 %copy.4 = f32[4,1024]{1,0:T(4,128)} copy(f32[4,1024]{1,0:T(4,128)} %shard_map.28) | data formatting | bytes 32768

commit v3 on v2

--- a/solution.py
+++ b/solution.py
@@ -91,23 +91,30 @@
     return rounded
 
 
-def shift(field, by):
-    return pltpu.roll(field, by % field.shape[1], 1)
-
-
-def smooth_x(field):
-    for _ in range(2):
-        field = field + shift(field, 1)
-        field = field + shift(field, -1)
-    return field
-
-
-def slope_x(field):
-    near = shift(field, -1) - shift(field, 1)
-    return 8.0 * near - (shift(near, 1) + shift(near, -1))
-
-
-def kernel(n, exchange, nx, raw_hbm, mats_hbm, out, raw, mats, send, halo, fields, *rest):
+def band(taps):
+    matrix = np.zeros((CELL + 2 * LANE, CELL))
+    for j in range(CELL):
+        for o, tap in enumerate(taps):
+            matrix[LANE + j + o - 2, j] = tap
+    return matrix
+
+
+def constants():
+    zy = np.pad(weights(), ((0, 0), (0, CELL - 192)))
+    along_x = np.concatenate([band(16.0 * smooth_taps), band(slope_taps)], axis=0)
+    return np.concatenate([zy, along_x.astype(ml_dtypes.bfloat16)], axis=0)
+
+
+def halves(field):
+    high = field.astype(jnp.bfloat16)
+    return high, (field - high.astype(jnp.float32)).astype(jnp.bfloat16)
+
+
+def dot(a, b):
+    return jnp.dot(a, b, preferred_element_type=jnp.float32)
+
+
+def kernel(n, exchange, nx, raw_hbm, mats_hbm, out, raw, mats, high, low, send, halo, fields, *rest):
     if exchange:
         staged, outbox, inbox, in_s, up_s, up_r, down_s, down_r, out_s, in_r = rest
     else:
@@ -149,9 +156,9 @@
                 send_sem=down_s.at[k], recv_sem=down_r.at[k], device_id=(down,), device_id_type=MESH),
         )
 
-    def filtered(rows, first):
-        window = raw[:, pl.ds(first, TILE + 2 * LANE)]
-        return smooth_x(jnp.dot(mats[rows, :], window, preferred_element_type=jnp.float32))[:, LANE:LANE + TILE]
+    def filtered(rows, lanes):
+        matrix = mats[rows, 0:192]
+        return dot(matrix, high[:, lanes]) + dot(matrix, low[:, lanes])
 
     def to_send(k, _):
         first = pl.multiple_of(k * TILE, TILE)
@@ -161,7 +168,12 @@
             for copy in inward[3:]:
                 copy.wait()
 
-        send[:, pl.ds(first, TILE)] = filtered(slice(0, 128), first).astype(jnp.bfloat16)
+        for cell in range(TILE // CELL):
+            at = pl.multiple_of(first + cell * CELL, CELL)
+            lanes = pl.ds(at, CELL)
+            high[:, lanes], low[:, lanes] = halves(dot(raw[:, pl.ds(at, CELL + 2 * LANE)], mats[512:1024, :]))
+        lanes = pl.ds(first, TILE)
+        send[:, lanes] = filtered(slice(0, 128), lanes).astype(jnp.bfloat16)
 
         @pl.when(k == 0)
         def _():
@@ -180,7 +192,7 @@
 
     def own(k, _):
         first = pl.multiple_of(k * TILE, TILE)
-        fields[:, pl.ds(first + LANE, TILE)] = filtered(slice(128, 320), first)
+        fields[:, pl.ds(first + LANE, TILE)] = filtered(slice(128, 320), pl.ds(first, TILE))
 
         @pl.when(k + FLIGHT < tiles)
         def _():
@@ -195,7 +207,7 @@
 
     def add_halo(k, _):
         first = pl.multiple_of(k * CELL, CELL)
-        more = jnp.dot(mats[320:512, :], halo[:, pl.ds(first, CELL)], preferred_element_type=jnp.float32)
+        more = dot(mats[320:512, 0:192], halo[:, pl.ds(first, CELL)])
         total = fields[:, pl.ds(first + LANE, CELL)] + more
         fields[:, pl.ds(first + LANE, CELL)] = total
 
@@ -214,14 +226,14 @@
 
     def shade(k, _):
         first = pl.multiple_of(lax.rem(k + 1, cells) * CELL, CELL)
+        slopes = sum(dot(half, mats[1024:1536, :]) for half in halves(fields[128:192, pl.ds(first, CELL + 2 * LANE)]))
         through = None
         for p in range(CZ):
             def centre(field):
                 return fields[field * 32 + p * BAND:field * 32 + (p + 1) * BAND, pl.ds(first + LANE, CELL)]
 
             def slope(field):
-                window = fields[field * 32 + p * BAND:field * 32 + (p + 1) * BAND, pl.ds(first, CELL + 2 * LANE)]
-                return slope_x(window)[:, LANE:LANE + CELL]
+                return slopes[(field - 4) * 32 + p * BAND:(field - 4) * 32 + (p + 1) * BAND]
 
             curl = centre(0)
             square = curl * curl
@@ -330,7 +342,9 @@
     bf16, f32 = jnp.bfloat16, jnp.float32
     scratch = [
         pltpu.VMEM((192, nx + 2 * LANE), bf16),
-        pltpu.VMEM((512, 192), bf16),
+        pltpu.VMEM((512 + 2 * (CELL + 2 * LANE), CELL), bf16),
+        pltpu.VMEM((192, nx), bf16),
+        pltpu.VMEM((192, nx), bf16),
         pltpu.VMEM((128, nx), bf16),
         pltpu.VMEM((2 * SIDE, nx), bf16),
         pltpu.VMEM((FIELDS * 32, nx + 2 * LANE), f32),
@@ -353,9 +367,9 @@
         out_specs=pl.BlockSpec(memory_space=pltpu.VMEM),
         scratch_shapes=scratch,
         compiler_params=pltpu.CompilerParams(
-            collective_id=0, has_side_effects=True, vmem_limit_bytes=60 * 1024 * 1024
+            collective_id=0, has_side_effects=True, vmem_limit_bytes=127 * 512 * 1024
         ),
-    )(velocity.reshape(3 * CZ * YH, nx), jnp.asarray(weights()))
+    )(velocity.reshape(3 * CZ * YH, nx), jnp.asarray(constants()))
     if exchange:
         return result
     parts = result.reshape(4, n, pixels).transpose(1, 0, 2).astype(bf16)

time: 34.9 us -> 34.1 us (0.977)
  Pallas kernels: 33.3 us -> 32.5 us
    pallas_call x1, Pallas kernels: 33.3 us -> 32.5 us  [per_device(): pl.pallas_call(functools.partial(kernel, n, exchange, nx), out_shape=jax....]
where the time goes in v3:
time: 34.1 us; the launch traced here: 33.9 us
  Pallas kernels  32.5 us (95%)
  local copies, waits for them, and re-layouts  1.32 us (4%)
    pallas_call x1, Pallas kernels, per_device(): pl.pallas_call(functools.partial(kernel, n, exchange, nx), out_shape=jax....  32.5 us
    unnamed x1, local copies, waits for them, and re-layouts  1.32 us

profile of v3, /device:TPU:3, one launch (start us, length us, event | category | flops | bytes accessed | tf_op | source)
XLA Modules:
  0.0 33.9 jit_solution(16239075788821949571)
XLA Ops:
  0.0 32.5 %shard_map.28 = f32[4,1024]{1,0:T(4,128)} custom-call(bf16[192,4096]{1,0:T(8,128)(2,1)} %bitcast.1, bf16[1536,256]{1,0:T(8,128)(2,1)} %constant.2.clone.mats_hbm), custom_call_target="tpu_custom_call" | custom-call | tf_op jit(solution)/shard_map/pallas_call | solution.py:363
  32.5 1.3 %copy.4 = f32[4,1024]{1,0:T(4,128)} copy(f32[4,1024]{1,0:T(4,128)} %shard_map.28) | data formatting | bytes 32768

commit v4 on v3

--- a/solution.py
+++ b/solution.py
@@ -105,16 +105,11 @@
     return np.concatenate([zy, along_x.astype(ml_dtypes.bfloat16)], axis=0)
 
 
-def halves(field):
-    high = field.astype(jnp.bfloat16)
-    return high, (field - high.astype(jnp.float32)).astype(jnp.bfloat16)
-
-
 def dot(a, b):
     return jnp.dot(a, b, preferred_element_type=jnp.float32)
 
 
-def kernel(n, exchange, nx, raw_hbm, mats_hbm, out, raw, mats, high, low, send, halo, fields, *rest):
+def kernel(n, exchange, nx, raw_hbm, mats_hbm, out, raw, mats, even, send, halo, fields, *rest):
     if exchange:
         staged, outbox, inbox, in_s, up_s, up_r, down_s, down_r, out_s, in_r = rest
     else:
@@ -156,10 +151,6 @@
                 send_sem=down_s.at[k], recv_sem=down_r.at[k], device_id=(down,), device_id_type=MESH),
         )
 
-    def filtered(rows, lanes):
-        matrix = mats[rows, 0:192]
-        return dot(matrix, high[:, lanes]) + dot(matrix, low[:, lanes])
-
     def to_send(k, _):
         first = pl.multiple_of(k * TILE, TILE)
 
@@ -171,9 +162,9 @@
         for cell in range(TILE // CELL):
             at = pl.multiple_of(first + cell * CELL, CELL)
             lanes = pl.ds(at, CELL)
-            high[:, lanes], low[:, lanes] = halves(dot(raw[:, pl.ds(at, CELL + 2 * LANE)], mats[512:1024, :]))
-        lanes = pl.ds(first, TILE)
-        send[:, lanes] = filtered(slice(0, 128), lanes).astype(jnp.bfloat16)
+            part = dot(raw[:, pl.ds(at, CELL + 2 * LANE)], mats[512:1024, :]).astype(jnp.bfloat16)
+            even[:, lanes] = part
+            send[:, lanes] = dot(mats[0:128, 0:192], part).astype(jnp.bfloat16)
 
         @pl.when(k == 0)
         def _():
@@ -190,25 +181,10 @@
         copy.wait()
     lax.fori_loop(0, tiles, to_send, 0)
 
-    def own(k, _):
-        first = pl.multiple_of(k * TILE, TILE)
-        fields[:, pl.ds(first + LANE, TILE)] = filtered(slice(128, 320), pl.ds(first, TILE))
-
-        @pl.when(k + FLIGHT < tiles)
-        def _():
-            for copy in halo_copies(k):
-                copy.wait_send()
-            for copy in halo_copies(k + FLIGHT):
-                copy.start()
-
-        return 0
-
-    lax.fori_loop(0, tiles, own, 0)
-
     def add_halo(k, _):
         first = pl.multiple_of(k * CELL, CELL)
-        more = dot(mats[320:512, 0:192], halo[:, pl.ds(first, CELL)])
-        total = fields[:, pl.ds(first + LANE, CELL)] + more
+        lanes = pl.ds(first, CELL)
+        total = dot(mats[128:320, 0:192], even[:, lanes]) + dot(mats[320:512, 0:192], halo[:, lanes])
         fields[:, pl.ds(first + LANE, CELL)] = total
 
         @pl.when(first == 0)
@@ -226,7 +202,7 @@
 
     def shade(k, _):
         first = pl.multiple_of(lax.rem(k + 1, cells) * CELL, CELL)
-        slopes = sum(dot(half, mats[1024:1536, :]) for half in halves(fields[128:192, pl.ds(first, CELL + 2 * LANE)]))
+        slopes = dot(fields[128:192, pl.ds(first, CELL + 2 * LANE)].astype(jnp.bfloat16), mats[1024:1536, :])
         through = None
         for p in range(CZ):
             def centre(field):
@@ -265,6 +241,14 @@
     def one_tile(k, _):
         for copy in halo_copies(k):
             copy.wait_recv()
+
+        @pl.when(k + FLIGHT < tiles)
+        def _():
+            for copy in halo_copies(k):
+                copy.wait_send()
+            for copy in halo_copies(k + FLIGHT):
+                copy.start()
+
         lax.fori_loop(k * per_tile, (k + 1) * per_tile, add_halo, 0)
         return 0
 
@@ -344,7 +328,6 @@
         pltpu.VMEM((192, nx + 2 * LANE), bf16),
         pltpu.VMEM((512 + 2 * (CELL + 2 * LANE), CELL), bf16),
         pltpu.VMEM((192, nx), bf16),
-        pltpu.VMEM((192, nx), bf16),
         pltpu.VMEM((128, nx), bf16),
         pltpu.VMEM((2 * SIDE, nx), bf16),
         pltpu.VMEM((FIELDS * 32, nx + 2 * LANE), f32),

time: 34.1 us -> 34 us (level)
  no operation moved by 1% of the time
where the time goes in v4:
time: 34 us; the launch traced here: 33.7 us
  Pallas kernels  32.4 us (95%)
  local copies, waits for them, and re-layouts  1.32 us (4%)
    pallas_call x1, Pallas kernels, per_device(): pl.pallas_call(functools.partial(kernel, n, exchange, nx), out_shape=jax....  32.4 us
    unnamed x1, local copies, waits for them, and re-layouts  1.32 us

profile of v4, /device:TPU:3, one launch (start us, length us, event | category | flops | bytes accessed | tf_op | source)
XLA Modules:
  0.0 33.7 jit_solution(10450408331949507024)
XLA Ops:
  0.0 32.4 %shard_map.28 = f32[4,1024]{1,0:T(4,128)} custom-call(bf16[192,4096]{1,0:T(8,128)(2,1)} %bitcast.1, bf16[1536,256]{1,0:T(8,128)(2,1)} %constant.2.clone.mats_hbm), custom_call_target="tpu_custom_call" | custom-call | tf_op jit(solution)/shard_map/pallas_call | solution.py:346
  32.4 1.3 %copy.4 = f32[4,1024]{1,0:T(4,128)} copy(f32[4,1024]{1,0:T(4,128)} %shard_map.28) | data formatting | bytes 32768

commit v5 on v4

--- a/solution.py
+++ b/solution.py
@@ -141,13 +141,12 @@
             pl.semaphore_signal(barrier, inc=1, device_id=(other,), device_id_type=MESH)
 
     def halo_copies(k):
-        lanes = pl.ds(pl.multiple_of(k * TILE, TILE), TILE)
         return (
             pltpu.make_async_remote_copy(
-                src_ref=send.at[pl.ds(0, SIDE), lanes], dst_ref=halo.at[pl.ds(0, SIDE), lanes],
+                src_ref=send.at[k, pl.ds(0, SIDE)], dst_ref=halo.at[k, pl.ds(0, SIDE)],
                 send_sem=up_s.at[k], recv_sem=up_r.at[k], device_id=(up,), device_id_type=MESH),
             pltpu.make_async_remote_copy(
-                src_ref=send.at[pl.ds(32, SIDE), lanes], dst_ref=halo.at[pl.ds(SIDE, SIDE), lanes],
+                src_ref=send.at[k, pl.ds(32, SIDE)], dst_ref=halo.at[k, pl.ds(SIDE, SIDE)],
                 send_sem=down_s.at[k], recv_sem=down_r.at[k], device_id=(down,), device_id_type=MESH),
         )
 
@@ -164,7 +163,7 @@
             lanes = pl.ds(at, CELL)
             part = dot(raw[:, pl.ds(at, CELL + 2 * LANE)], mats[512:1024, :]).astype(jnp.bfloat16)
             even[:, lanes] = part
-            send[:, lanes] = dot(mats[0:128, 0:192], part).astype(jnp.bfloat16)
+            send[k, :, cell * CELL:(cell + 1) * CELL] = dot(mats[0:128, 0:192], part).astype(jnp.bfloat16)
 
         @pl.when(k == 0)
         def _():
@@ -181,10 +180,11 @@
         copy.wait()
     lax.fori_loop(0, tiles, to_send, 0)
 
-    def add_halo(k, _):
-        first = pl.multiple_of(k * CELL, CELL)
+    def add_halo(tile, cell):
+        first = pl.multiple_of(tile * TILE + cell * CELL, CELL)
         lanes = pl.ds(first, CELL)
-        total = dot(mats[128:320, 0:192], even[:, lanes]) + dot(mats[320:512, 0:192], halo[:, lanes])
+        arrived_cell = halo[tile, :, cell * CELL:(cell + 1) * CELL]
+        total = dot(mats[128:320, 0:192], even[:, lanes]) + dot(mats[320:512, 0:192], arrived_cell)
         fields[:, pl.ds(first + LANE, CELL)] = total
 
         @pl.when(first == 0)
@@ -194,8 +194,6 @@
         @pl.when(first == nx - CELL)
         def _():
             fields[128:192, 0:LANE] = total[128:192, CELL - LANE:CELL]
-
-        return 0
 
     scale = opacity_gain / (144.0 * CZ * n)
     per_chunk = CHUNK // CELL
@@ -236,8 +234,6 @@
                 staged[pl.ds(pl.multiple_of(row * BAND, BAND), BAND), :] = part[:, j * LANE:(j + 1) * LANE]
         return 0
 
-    per_tile = TILE // CELL
-
     def one_tile(k, _):
         for copy in halo_copies(k):
             copy.wait_recv()
@@ -249,7 +245,8 @@
             for copy in halo_copies(k + FLIGHT):
                 copy.start()
 
-        lax.fori_loop(k * per_tile, (k + 1) * per_tile, add_halo, 0)
+        for cell in range(TILE // CELL):
+            add_halo(k, cell)
         return 0
 
     def one_chunk(c, _):
@@ -261,7 +258,8 @@
         for r in range(BAND):
             outbox[c * BAND + r] = staged[pl.ds(r, 32, stride=BAND), :].astype(jnp.bfloat16)
 
-        def post(r, _):
+        def post(i, _):
+            r = lax.rem(i + me // chunks, BAND)
             owner = r * chunks + c
 
             @pl.when(owner != me)
@@ -328,8 +326,8 @@
         pltpu.VMEM((192, nx + 2 * LANE), bf16),
         pltpu.VMEM((512 + 2 * (CELL + 2 * LANE), CELL), bf16),
         pltpu.VMEM((192, nx), bf16),
-        pltpu.VMEM((128, nx), bf16),
-        pltpu.VMEM((2 * SIDE, nx), bf16),
+        pltpu.VMEM((tiles, 128, TILE), bf16),
+        pltpu.VMEM((tiles, 2 * SIDE, TILE), bf16),
         pltpu.VMEM((FIELDS * 32, nx + 2 * LANE), f32),
     ]
     if exchange:
@@ -350,7 +348,7 @@
         out_specs=pl.BlockSpec(memory_space=pltpu.VMEM),
         scratch_shapes=scratch,
         compiler_params=pltpu.CompilerParams(
-            collective_id=0, has_side_effects=True, vmem_limit_bytes=127 * 512 * 1024
+            collective_id=0, has_side_effects=True, vmem_limit_bytes=53 * 1024 * 1024
         ),
     )(velocity.reshape(3 * CZ * YH, nx), jnp.asarray(constants()))
     if exchange:

time: 34 us -> 34.1 us (level)
  local copies, waits for them, and re-layouts: 1.32 us -> 1.74 us
    unnamed x1 -> x3, local copies, waits for them, and re-layouts: 1.32 us -> 1.74 us
where the time goes in v5:
time: 34.1 us; the launch traced here: 34 us
  Pallas kernels  32.2 us (94%)
  local copies, waits for them, and re-layouts  1.74 us (5%)
    pallas_call x1, Pallas kernels, per_device(): pl.pallas_call(functools.partial(kernel, n, exchange, nx), out_shape=jax....  32.2 us
    unnamed x3, local copies, waits for them, and re-layouts  1.74 us

profile of v5, /device:TPU:3, one launch (start us, length us, event | category | flops | bytes accessed | tf_op | source)
XLA Modules:
  0.0 34.0 jit_solution(13169235805083914981)
XLA Ops:
  0.0 0.0 copy-start
  0.0 1.1 %copy-done = bf16[1536,256]{1,0:T(8,128)(2,1)S(1)} copy-done((bf16[1536,256]{1,0:T(8,128)(2,1)S(1)}, bf16[1536,256]{1,0:T(8,128)(2,1)}, u32[]{:S(2)}) %copy-start) | copy-done | bytes 786456
  1.1 32.2 %shard_map.28 = f32[4,1024]{1,0:T(4,128)S(1)} custom-call(bf16[192,4096]{1,0:T(8,128)(2,1)} %bitcast.1, bf16[1536,256]{1,0:T(8,128)(2,1)S(1)} %copy-done), custom_call_target="tpu_custom_call" | custom-call | tf_op jit(solution)/shard_map/pallas_call | solution.py:344
  33.4 0.6 %copy.4 = f32[4,1024]{1,0:T(4,128)} copy(f32[4,1024]{1,0:T(4,128)S(1)} %shard_map.28) | data formatting | bytes 32768
Async XLA Ops:
  0.0 1.1 %copy-start = (bf16[1536,256]{1,0:T(8,128)(2,1)S(1)}, bf16[1536,256]{1,0:T(8,128)(2,1)}, u32[]{:S(2)}) copy-start(bf16[1536,256]{1,0:T(8,128)(2,1)} %constant.2.clone.mats_hbm) | copy-start | bytes 2359300
